TPU v7x, 1024 devices: a whole 4x8x16 slice. The times are simulated.
1024 devices in a mesh: row: 64 (over y, x, core), col: 16 (over z).
Axes of the slice: x: 4, y: 8, z: 16, core: 2. Of those that a mesh axis runs over, the one named last changes fastest.
Arguments:
- user_factors: bfloat16 [131072, 256], P(('row', 'col')), may hold values from -0.375 to 0.375
- item_factors: float32 [262144, 256], P(('row', 'col')), may hold values from -4 to 4
- send_rows: int32 [65536, 16], P(('row', 'col')), may hold values from 0 to 127, as said below
- tile_users: int32 [8192, 128], P(('row', 'col')), may hold values from 0 to 1023
- tile_block: int32 [8192], P(('row', 'col')), may hold values from 0 to 1
- tile_counts: int32 [8192, 128, 128], P(('row', 'col')), may hold values from 0 to 7
- tile_live: int32 [64, 16], P('row', 'col'), may hold values from 4 to 8, as said below
Outputs:
- new_items: float32 [262144, 256], P(('row', 'col'))
Inputs may be any that keep to these rules, and one draw needn't show every extreme that they name: `send_rows`: each row of a device's list for one destination holds distinct local user rows. `tile_live`: at least half of the slots are live; some device has all 8 live.
All inputs are finite; a program needn't handle non-finite values.
Results may differ from a plain program's by a relative error of at most 0.0007.
Values may be sent and summed in bfloat16 or wider, within the bound.
A program may use at most 32 MiB of HBM per device.

v0:
```python
import jax
import jax.numpy as jnp
from jax import lax
from jax.sharding import PartitionSpec as P

ITERS = 3


HI = lax.Precision.HIGHEST


def item_solve(gram, recv, users_idx, blocks, counts, live, start):
    tiles = users_idx.shape[0]
    side = users_idx.shape[1]
    nblocks = start.shape[0] // side
    width = start.shape[1]
    tile_rows = recv[users_idx].astype(jnp.float32)
    alive = (jnp.arange(tiles, dtype=jnp.int32) < live).astype(jnp.float32)
    conf = 40.0 * counts.astype(jnp.float32) * alive[:, None, None]
    pref = (counts > 0).astype(jnp.float32) * alive[:, None, None]
    onehot = (blocks[:, None] == jnp.arange(nblocks, dtype=jnp.int32)[None, :]).astype(jnp.float32)

    def back(contrib):
        return jnp.einsum("tk,tif->kif", onehot, contrib, precision=HI).reshape(
            nblocks * side, width
        )

    def hessian(field):
        per_tile = jnp.einsum(
            "tk,kif->tif", onehot, field.reshape(nblocks, side, width), precision=HI
        )
        scores = jnp.einsum("tif,tuf->tiu", per_tile, tile_rows, precision=HI)
        contrib = jnp.einsum("tiu,tuf->tif", conf * scores, tile_rows, precision=HI)
        return jnp.dot(field, gram, precision=HI) + 0.1 * field + back(contrib)

    rhs = back(jnp.einsum("tiu,tuf->tif", (1.0 + conf) * pref, tile_rows, precision=HI))
    solution = start
    resid = rhs - hessian(solution)
    direction = resid
    norm_now = jnp.sum(resid * resid, axis=1, keepdims=True)
    for step in range(ITERS):
        image = hessian(direction)
        alpha = norm_now / jnp.sum(direction * image, axis=1, keepdims=True)
        solution = solution + alpha * direction
        resid = resid - alpha * image
        norm_next = jnp.sum(resid * resid, axis=1, keepdims=True)
        direction = resid + norm_next / norm_now * direction
        norm_now = norm_next
    return solution


def sum_gram(local_gram):
    return lax.psum(local_gram, ("row", "col"))


def body(user_factors, item_factors, send_rows, tile_users, tile_block, tile_counts, tile_live):
    local_gram = jnp.dot(user_factors.T, user_factors, preferred_element_type=jnp.float32)
    gram = sum_gram(local_gram)
    groups = lax.axis_size("row")
    slots = send_rows.shape[1]
    outgoing = user_factors[send_rows]
    arrived = lax.all_to_all(outgoing, "row", split_axis=0, concat_axis=0, tiled=True)
    received = arrived.reshape(groups * slots, user_factors.shape[1])
    return item_solve(
        gram, received, tile_users, tile_block, tile_counts, tile_live[0, 0], item_factors
    )


def solution(mesh):
    in_specs = (
        P(("row", "col"), None),
        P(("row", "col"), None),
        P(("row", "col"), None),
        P(("row", "col"), None),
        P(("row", "col")),
        P(("row", "col"), None, None),
        P("row", "col"),
    )
    out_specs = P(("row", "col"), None)
    return jax.shard_map(body, mesh=mesh, in_specs=in_specs, out_specs=out_specs, check_vma=False)
```

profile of v0, /device:TPU:1, one launch (start us, length us, event | category | flops | bytes accessed | tf_op | source)
XLA Modules:
  0.0 536.3 jit_solution(2267451792273171695)
XLA Ops:
  6.5 0.7 compare_select_fusion
  7.5 4.9 gather_fusion
  12.4 18.2 %all-to-all-start = ((bf16[64,16,256]{2,1,0:T(8,128)(2,1)}), bf16[64,16,256]{2,1,0:T(8,128)(2,1)S(1)}, u32[]{:S(2)}, u32[]{:S(2)}) async-start(bf16[64,16,256]{2,1,0:T(8,128)(2,1)} %bitcast.2), calls=%async_computation | async-start | bytes 1048576 | tf_op jit(solution)/shard_map/all_to_all | solution.py:62
  30.7 0.9 fusion.63
  32.3 0.7 copy-done.5
  33.6 0.8 fusion.33
  34.4 14.0 %all-to-all-done = bf16[64,16,256]{2,1,0:T(8,128)(2,1)S(1)} async-done(((bf16[64,16,256]{2,1,0:T(8,128)(2,1)}), bf16[64,16,256]{2,1,0:T(8,128)(2,1)S(1)}, u32[]{:S(2)}, u32[]{:S(2)}) %all-to-all-start) | async-done | bytes 524320 | tf_op jit(solution)/shard_map/all_to_all | solution.py:62
  48.5 4.1 gather_fusion.1
  53.2 1.2 fusion.20
  54.4 0.9 convolution_multiply_fusion.3
  55.9 1.2 fusion.17
  57.1 456.4 %all-reduce.2.cloned.1.call-done = f32[256,256]{1,0:T(8,128)} async-done(((f32[256,256]{1,0:T(8,128)}), f32[256,256]{1,0:T(8,128)}) %all-reduce.2.cloned.1.call-update) | async-done | bytes 262160 | tf_op jit(solution)/shard_map/psum | solution.py:53
  513.5 1.3 fusion.6
  514.9 0.8 fusion.31
  515.7 0.9 convolution_multiply_fusion.2
  517.1 1.2 fusion.14
  518.3 0.9 copy-done.2
  520.1 0.8 fusion.29
  520.9 0.9 convolution_multiply_fusion.1
  522.4 1.4 fusion.11
  524.6 0.8 fusion.27
  525.4 0.9 convolution_multiply_fusion
  526.9 1.2 fusion.8
  528.5 0.9 multiply_add_fusion
  (40 shorter events, 6.0 us)
Async XLA Ops:
  6.5 0.9 copy-start
  12.4 36.1 %all-to-all-start = ((bf16[64,16,256]{2,1,0:T(8,128)(2,1)}), bf16[64,16,256]{2,1,0:T(8,128)(2,1)S(1)}, u32[]{:S(2)}, u32[]{:S(2)}) async-start(bf16[64,16,256]{2,1,0:T(8,128)(2,1)} %bitcast.2), calls=%async_computation | async-start | bytes 1048576 | tf_op jit(solution)/shard_map/all_to_all | solution.py:62
  30.6 2.3 copy-start.3
  30.6 482.9 %all-reduce.2.cloned.1.call-start = ((), (), s32[]{:S(2)}) async-start(), calls=%async_computation.1 | async-start | bytes 524288 | tf_op jit(solution)/shard_map/psum | solution.py:53
  32.3 0.7 copy-start.5
  33.0 0.7 copy-start.4
  48.5 4.1 copy-start.1
  518.3 1.0 copy-start.2
Sparse Core Ops, SparseCore 0:
  36.9 476.5 all-reduce.1
where the time goes:
time: 538 us; the launch traced here: 536 us
  waiting for transfers between devices  470 us (87%)
  matrix products  19.3 us (4%)
  starting transfers between devices  18.3 us (3%)
  between operations  14.3 us (3%)
  local copies, waits for them, and re-layouts  11.6 us (2%)
    psum x1, waiting for transfers between devices, sum_gram(): return lax.psum(local_gram, ('row', 'col'))  456 us
    all_to_all x1, starting transfers between devices, body(): lax.all_to_all(outgoing, 'row', split_axis=0, concat_axis=0, tiled=True)  18.2 us
    all_to_all x1, waiting for transfers between devices, body(): lax.all_to_all(outgoing, 'row', split_axis=0, concat_axis=0, tiled=True)  14 us
  transfers between devices with their start and end apart: 2, of which 2 were waited for; matrix products, arithmetic and copies ran while one was open for 2% of the time, Pallas kernels for 0%

commit v1 on v0

v1 whole, which is shorter than its diff:
```python
import functools

import jax
import jax.numpy as jnp
from jax import lax
from jax.experimental import pallas as pl
from jax.experimental.pallas import tpu as pltpu
from jax.sharding import PartitionSpec as P

ITERS = 3
CORES_X = 8
MESH = pl.DeviceIdType.MESH
F32 = jnp.float32
BF16 = jnp.bfloat16

NN = (((1,), (0,)), ((), ()))
NT = (((1,), (1,)), ((), ()))
TN = (((0,), (0,)), ((), ()))


def dot(a, b, dims=NN):
    return lax.dot_general(a, b, dims, preferred_element_type=F32)


def split(x):
    high = x.astype(BF16)
    return high, (x - high.astype(F32)).astype(BF16)


def kernel(
    n_row, n_col, side,
    users_ref, items_ref, send_ref, tile_users_ref, tile_block_ref, counts_ref, live_ref,
    out_ref,
    outgoing, recv, local, s1, p1, s2, p2, s3, s4, full, hot, left, conf, rh, rl,
    row_send, row_recv, send_sems, recv_sems,
):
    r = lax.axis_index("row")
    c = lax.axis_index("col")
    nj = side
    ny = n_row // nj
    j = lax.rem(r, nj)
    y = lax.div(r, nj)
    tiles_j = s1.shape[1]
    tiles_y = s2.shape[1]
    rows_dev, width = users_ref.shape
    slots = send_ref.shape[1]
    n_recv = n_row * slots

    barrier = pltpu.get_barrier_semaphore()

    def greet_row(k, carry):
        pl.semaphore_signal(barrier, inc=1, device_id=(lax.rem(r + k, n_row), c), device_id_type=MESH)
        return carry

    def greet_col(k, carry):
        pl.semaphore_signal(barrier, inc=1, device_id=(r, lax.rem(c + k, n_col)), device_id_type=MESH)
        return carry

    lax.fori_loop(1, n_row, greet_row, 0)
    lax.fori_loop(1, n_col, greet_col, 0)

    u = users_ref[...]
    gram = dot(u, u, TN)
    for a in range(width // 8):
        for h in range(width // 128):
            local[a * (width // 128) + h] = gram[8 * a:8 * a + 8, 128 * h:128 * h + 128]

    wanted = send_ref[...][:, :, None]
    pick = (wanted == lax.broadcasted_iota(jnp.int32, (n_row, slots, rows_dev), 2)).astype(F32)
    rows_out = dot(pick.reshape(n_recv, rows_dev).astype(BF16), u).astype(BF16)
    outgoing[...] = rows_out.reshape(n_row, slots, width)

    pl.semaphore_wait(barrier, n_row - 1 + n_col - 1)

    def stage(index, count, source, target, device):
        def one(k, carry):
            pltpu.make_async_remote_copy(
                src_ref=source(k), dst_ref=target, send_sem=send_sems.at[index], recv_sem=recv_sems.at[index],
                device_id=device(k), device_id_type=MESH,
            ).start()
            return carry

        lax.fori_loop(1, count, one, 0)

    def arrived(index, buffer, count):
        view = buffer.at[pl.ds(0, count - 1)]
        pltpu.make_async_copy(view, view, recv_sems.at[index]).wait()

    def peer_j(k):
        return lax.rem(j + k, nj)

    def peer_y(k):
        return lax.rem(y + k, ny)

    def peer_z(k):
        return lax.rem(c + k, n_col)

    stage(0, nj, lambda k: local.at[pl.ds(peer_j(k) * tiles_j, tiles_j)], s1.at[j],
          lambda k: (y * nj + peer_j(k), c))

    def send_row(k, carry):
        peer = lax.rem(r + k, n_row)
        pltpu.make_async_remote_copy(
            src_ref=outgoing.at[peer], dst_ref=recv.at[r], send_sem=row_send, recv_sem=row_recv,
            device_id=(peer, c), device_id_type=MESH,
        ).start()
        return carry

    lax.fori_loop(1, n_row, send_row, 0)
    recv[r] = outgoing[r]
    s1[j] = local[pl.ds(j * tiles_j, tiles_j)]

    tiles = tile_users_ref.shape[0]
    block = tile_users_ref.shape[1]
    blocks = items_ref.shape[0] // block
    for t in range(tiles):
        row = tile_users_ref[t:t + 1, :]
        hit = lax.broadcasted_iota(jnp.int32, (n_recv, block), 0) == row
        hot[:, t * block:(t + 1) * block] = hit.astype(F32).astype(BF16)

    arrived(0, s1, nj)
    total = s1[0]
    for k in range(1, nj):
        total = total + s1[k]
    p1[...] = total

    stage(1, ny, lambda k: p1.at[pl.ds(peer_y(k) * tiles_y, tiles_y)], s2.at[y],
          lambda k: (peer_y(k) * nj + j, c))
    s2[y] = p1[pl.ds(y * tiles_y, tiles_y)]

    live = live_ref[0, 0]
    half = blocks * block
    for t in range(tiles):
        counts = counts_ref[t].astype(F32)
        pref = (counts > 0).astype(F32)
        alive = (t < live).astype(F32)
        for k in range(blocks):
            mine = (tile_block_ref[t] == k).astype(F32) * alive
            left[k * block:(k + 1) * block, t * block:(t + 1) * block] = (counts * mine).astype(BF16)
            left[half + k * block:half + (k + 1) * block, t * block:(t + 1) * block] = (pref * mine).astype(BF16)

    arrived(1, s2, ny)
    total = s2[0]
    for k in range(1, ny):
        total = total + s2[k]
    p2[...] = total

    stage(2, n_col, lambda k: p2, s3.at[c], lambda k: (r, peer_z(k)))
    s3[c] = p2[...]

    sums = dot(left[...], hot[...], NT)
    conf_all = 40.0 * sums[:half]
    conf[...] = conf_all
    high, low = split(sums[half:] + conf_all)
    rh[...] = high
    rl[...] = low

    arrived(2, s3, n_col)
    total = s3[0]
    for k in range(1, n_col):
        total = total + s3[k]
    s4[y] = total

    stage(3, ny, lambda k: s4.at[y], s4.at[y], lambda k: (peer_y(k) * nj + j, c))
    arrived(3, s4, ny)

    stage(4, nj, lambda k: s4, full.at[j], lambda k: (y * nj + peer_j(k), c))
    full[j] = s4[...]

    view = recv.at[pl.ds(0, n_row - 1)]
    pltpu.make_async_copy(view, view, row_recv).wait()

    rows = recv[...].reshape(n_recv, width)

    def tile_part(parts):
        vh, vl = parts
        scores = dot(vh, rows, NT) + dot(vl, rows, NT)
        wh, wl = split(conf[...] * scores)
        return dot(wh, rows) + dot(wl, rows)

    start = items_ref[...]
    parts = split(start)
    resid = dot(rh[...], rows) + dot(rl[...], rows) - tile_part(parts) - 0.1 * start

    arrived(4, full, nj)
    strips = []
    per = width // 128
    for a in range(width // 8):
        cells = [full[(a * per + h) // tiles_j, ((a * per + h) % tiles_j) // tiles_y, (a * per + h) % tiles_y] for h in range(per)]
        strips.append(jnp.concatenate(cells, axis=1))
    gh, gl = split(jnp.concatenate(strips, axis=0))

    def gram_part(parts):
        vh, vl = parts
        return dot(vh, gh) + dot(vl, gh) + dot(vh, gl)

    resid = resid - gram_part(parts)
    solution = start
    direction = resid
    norm_now = jnp.sum(resid * resid, axis=1, keepdims=True)
    for step in range(ITERS):
        parts = split(direction)
        image = tile_part(parts) + gram_part(parts) + 0.1 * direction
        alpha = norm_now / jnp.sum(direction * image, axis=1, keepdims=True)
        solution = solution + alpha * direction
        if step < ITERS - 1:
            resid = resid - alpha * image
            norm_next = jnp.sum(resid * resid, axis=1, keepdims=True)
            direction = resid + norm_next / norm_now * direction
            norm_now = norm_next
    out_ref[...] = solution

    view = outgoing.at[pl.ds(0, n_row - 1)]
    pltpu.make_async_copy(view, view, row_send).wait()
    for index, (buffer, count) in enumerate(((s1, nj), (s2, ny), (s3, n_col), (s4, ny), (full, nj))):
        view = buffer.at[pl.ds(0, count - 1)]
        pltpu.make_async_copy(view, view, send_sems.at[index]).wait()


def body(n_row, n_col, side, user_factors, item_factors, send_rows, tile_users, tile_block, tile_counts, tile_live):
    rows_dev, width = user_factors.shape
    slots = send_rows.shape[1]
    ny = n_row // side
    n_tiles = width // 8 * (width // 128)
    tiles_j = n_tiles // side
    tiles_y = tiles_j // ny
    n_recv = n_row * slots
    columns = tile_users.shape[0] * tile_users.shape[1]
    items = item_factors.shape[0]
    vmem = pl.BlockSpec(memory_space=pltpu.VMEM)
    smem = pl.BlockSpec(memory_space=pltpu.SMEM)
    return pl.pallas_call(
        functools.partial(kernel, n_row, n_col, side),
        out_shape=jax.ShapeDtypeStruct(item_factors.shape, F32),
        in_specs=[vmem, vmem, vmem, vmem, smem, vmem, smem],
        out_specs=vmem,
        scratch_shapes=[
            pltpu.VMEM((n_row, slots, width), BF16),
            pltpu.VMEM((n_row, slots, width), BF16),
            pltpu.VMEM((n_tiles, 8, 128), F32),
            pltpu.VMEM((side, tiles_j, 8, 128), F32),
            pltpu.VMEM((tiles_j, 8, 128), F32),
            pltpu.VMEM((ny, tiles_y, 8, 128), F32),
            pltpu.VMEM((tiles_y, 8, 128), F32),
            pltpu.VMEM((n_col, tiles_y, 8, 128), F32),
            pltpu.VMEM((ny, tiles_y, 8, 128), F32),
            pltpu.VMEM((side, ny, tiles_y, 8, 128), F32),
            pltpu.VMEM((n_recv, columns), BF16),
            pltpu.VMEM((2 * items, columns), BF16),
            pltpu.VMEM((items, n_recv), F32),
            pltpu.VMEM((items, n_recv), BF16),
            pltpu.VMEM((items, n_recv), BF16),
            pltpu.SemaphoreType.DMA,
            pltpu.SemaphoreType.DMA,
            pltpu.SemaphoreType.DMA((5,)),
            pltpu.SemaphoreType.DMA((5,)),
        ],
        compiler_params=pltpu.CompilerParams(
            collective_id=0, has_side_effects=True, vmem_limit_bytes=48 * 1024 * 1024
        ),
    )(user_factors, item_factors, send_rows, tile_users, tile_block, tile_counts, tile_live)


def solution(mesh):
    n_row, n_col = mesh.shape["row"], mesh.shape["col"]
    in_specs = (
        P(("row", "col"), None),
        P(("row", "col"), None),
        P(("row", "col"), None),
        P(("row", "col"), None),
        P(("row", "col")),
        P(("row", "col"), None, None),
        P("row", "col"),
    )
    return jax.shard_map(
        functools.partial(body, n_row, n_col, min(CORES_X, n_row // 2)),
        mesh=mesh, in_specs=in_specs, out_specs=P(("row", "col"), None), check_vma=False,
    )
```

time: 538 us -> 67 us (0.12)
  waiting for transfers between devices: 470 us -> 0 us
  Pallas kernels: 0 us -> 61.7 us
  matrix products: 19.3 us -> 0 us
  starting transfers between devices: 18.3 us -> 0 us
  between operations: 14.3 us -> 0.69 us
  local copies, waits for them, and re-layouts: 11.6 us -> 4.33 us
    psum x1 -> x0, waiting for transfers between devices: 456 us -> none  [sum_gram(): return lax.psum(local_gram, ('row', 'col'))]
    pallas_call x0 -> x1, Pallas kernels: none -> 61.7 us  [body(): pl.pallas_call(functools.partial(kernel, n_row, n_col, side), out_shape=j...]
    dot_general x23 -> x0, matrix products: 19.3 us -> none  [the longest x5 6.05 us: back(): jnp.einsum('tk,tif->kif', onehot, contrib, precision=HI)]
    all_to_all x1 -> x0, starting transfers between devices: 18.2 us -> none  [body(): lax.all_to_all(outgoing, 'row', split_axis=0, concat_axis=0, tiled=True)]
    all_to_all x1 -> x0, waiting for transfers between devices: 14 us -> none  [body(): lax.all_to_all(outgoing, 'row', split_axis=0, concat_axis=0, tiled=True)]
    gather x2 -> x0, local copies, waits for them, and re-layouts: 9.06 us -> none  [the longest x1 4.95 us: body(): outgoing = user_factors[send_rows]]
  transfers between devices with their start and end apart: 2 -> 0, of which waited for: 2 -> 0; matrix products, arithmetic and copies ran while one was open for 2% -> 0% of each run, Pallas kernels for 0% -> 0%
where the time goes in v1:
time: 67 us; the launch traced here: 66.7 us
  Pallas kernels  61.7 us (92%)
  local copies, waits for them, and re-layouts  4.33 us (6%)
  between operations  0.69 us (1%)
    pallas_call x1, Pallas kernels, body(): pl.pallas_call(functools.partial(kernel, n_row, n_col, side), out_shape=j...  61.7 us
    unnamed x12, local copies, waits for them, and re-layouts  4.33 us

profile of v1, /device:TPU:1, one launch (start us, length us, event | category | flops | bytes accessed | tf_op | source)
XLA Modules:
  0.0 66.7 jit_solution(7148303836117590843)
XLA Ops:
  0.7 0.0 copy-start.3
  0.7 0.0 copy-start.4
  0.7 0.8 %copy.8.send_ref = s32[64,16]{1,0:T(8,128)S(1)} copy(s32[64,16]{0,1:T(8,128)} %param.9) | data formatting | bytes 8192 | tf_op args[2]
  1.5 0.0 copy-done.3
  1.5 0.0 copy-done.4
  1.5 0.0 copy-start
  1.5 1.0 %copy-done = s32[8,128,128]{2,1,0:T(8,128)S(1)} copy-done((s32[8,128,128]{2,1,0:T(8,128)S(1)}, s32[8,128,128]{2,1,0:T(8,128)}, u32[]{:S(2)}) %copy-start) | copy-done | bytes 524312
  2.5 0.0 copy-start.1
  2.5 0.9 %copy-done.1 = f32[256,256]{1,0:T(8,128)S(1)} copy-done((f32[256,256]{1,0:T(8,128)S(1)}, f32[256,256]{1,0:T(8,128)}, u32[]{:S(2)}) %copy-start.1) | copy-done | bytes 262168
  3.5 0.0 copy-start.2
  3.5 0.8 %copy-done.2 = bf16[128,256]{1,0:T(8,128)(2,1)S(1)} copy-done((bf16[128,256]{1,0:T(8,128)(2,1)S(1)}, bf16[128,256]{1,0:T(8,128)(2,1)}, u32[]{:S(2)}) %copy-start.2) | copy-done | bytes 65560
  4.3 61.7 %shard_map.73 = f32[256,256]{1,0:T(8,128)S(1)} custom-call(bf16[128,256]{1,0:T(8,128)(2,1)S(1)} %copy-done.2, f32[256,256]{1,0:T(8,128)S(1)} %copy-done.1, s32[64,16]{1,0:T(8,128)S(1)} %copy.8.send_ref, s32[8,128]{1,0:T(8,128)S(1)} %copy-done.3, s32[8]{0:T(128)S(1)} %copy-done.4, s32[8,128,128]{2,1,0:T(8,128)S(1)} %copy-done, s32[1,1]{1,0:T(1,128)S(6)} %copy.10.live_ref), custom_call_target="tpu_custom_call" | custom-call | tf_op jit(solution)/shard_map/pallas_call | solution.py:232
  66.0 0.7 %copy.11 = f32[256,256]{1,0:T(8,128)} copy(f32[256,256]{1,0:T(8,128)S(1)} %shard_map.73) | data formatting | bytes 524288
Async XLA Ops:
  0.7 0.8 %copy-start.3 = (s32[8,128]{1,0:T(8,128)S(1)}, s32[8,128]{1,0:T(8,128)}, u32[]{:S(2)}) copy-start(s32[8,128]{1,0:T(8,128)} %tile_users_ref.1) | copy-start | bytes 12292
  0.7 0.8 %copy-start.4 = (s32[8]{0:T(128)S(1)}, s32[8]{0:T(128)}, u32[]{:S(2)}) copy-start(s32[8]{0:T(128)} %tile_block_ref.1) | copy-start | bytes 100
  1.5 1.0 %copy-start = (s32[8,128,128]{2,1,0:T(8,128)S(1)}, s32[8,128,128]{2,1,0:T(8,128)}, u32[]{:S(2)}) copy-start(s32[8,128,128]{2,1,0:T(8,128)} %counts_ref.1) | copy-start | bytes 1572868
  2.5 0.9 %copy-start.1 = (f32[256,256]{1,0:T(8,128)S(1)}, f32[256,256]{1,0:T(8,128)}, u32[]{:S(2)}) copy-start(f32[256,256]{1,0:T(8,128)} %items_ref.1) | copy-start | bytes 786436
  3.5 0.8 %copy-start.2 = (bf16[128,256]{1,0:T(8,128)(2,1)S(1)}, bf16[128,256]{1,0:T(8,128)(2,1)}, u32[]{:S(2)}) copy-start(bf16[128,256]{1,0:T(8,128)(2,1)} %users_ref.1) | copy-start | bytes 196612

commit v2 on v1

v2 whole, which is shorter than its diff:
```python
import functools

import jax
import jax.numpy as jnp
from jax import lax
from jax.experimental import pallas as pl
from jax.experimental.pallas import tpu as pltpu
from jax.sharding import PartitionSpec as P

ITERS = 3
MESH = pl.DeviceIdType.MESH
F32 = jnp.float32
BF16 = jnp.bfloat16

NN = (((1,), (0,)), ((), ()))
NT = (((1,), (1,)), ((), ()))
TN = (((0,), (0,)), ((), ()))


def dot(a, b, dims=NN):
    return lax.dot_general(a, b, dims, preferred_element_type=F32)


def split(x):
    high = x.astype(BF16)
    return high, (x - high.astype(F32)).astype(BF16)


def far_first(n):
    return sorted(range(1, n), key=lambda k: -min(k, n - k))


def kernel(
    dims,
    users_hbm, items_hbm, wanted_hbm, tile_users_hbm, tile_block_hbm, counts_hbm, live_hbm,
    out_ref,
    users_ref, items_ref, wanted_ref, tile_users_ref, tile_block_ref, counts_ref, live_ref,
    outgoing, recv, local, s0, p0, s1, p1, s2, p2, s3, s4, full, hot, left, conf, rh, rl,
    load_sems, row_send, row_recv, send_sems, recv_sems,
):
    ny, nx, n_col = dims
    n_row = ny * nx * 2
    r = lax.axis_index("row")
    c = lax.axis_index("col")
    core = lax.rem(r, 2)
    x = lax.rem(lax.div(r, 2), nx)
    y = lax.div(r, 2 * nx)
    rows_dev, width = users_ref.shape
    slots = wanted_ref.shape[0]
    n_recv = n_row * slots

    barrier = pltpu.get_barrier_semaphore()
    for k in far_first(n_col):
        pl.semaphore_signal(barrier, inc=1, device_id=(r, lax.rem(c + k, n_col)), device_id_type=MESH)

    def greet_row(k, carry):
        pl.semaphore_signal(barrier, inc=1, device_id=(lax.rem(r + k, n_row), c), device_id_type=MESH)
        return carry

    loads = [
        pltpu.make_async_copy(source, target, load_sems.at[i])
        for i, (source, target) in enumerate((
            (users_hbm, users_ref), (wanted_hbm, wanted_ref), (items_hbm, items_ref), (tile_users_hbm, tile_users_ref),
            (tile_block_hbm, tile_block_ref), (live_hbm, live_ref), (counts_hbm, counts_ref),
        ))
    ]
    for load in loads:
        load.start()
    lax.fori_loop(1, n_row, greet_row, 0)
    loads[0].wait()
    loads[1].wait()

    per = width // 128
    u = users_ref[...]
    gram = dot(u, u, TN)
    for a in range(width // 8):
        for h in range(per):
            local[a * per + h] = gram[8 * a:8 * a + 8, 128 * h:128 * h + 128]

    wanted = wanted_ref[...].T[:, :, None]
    pick = (wanted == lax.broadcasted_iota(jnp.int32, (n_row, slots, rows_dev), 2)).astype(F32)
    rows_out = dot(pick.reshape(n_recv, rows_dev).astype(BF16), u).astype(BF16)
    outgoing[...] = rows_out.reshape(n_row, slots, width)

    pl.semaphore_wait(barrier, n_row - 1 + n_col - 1)

    def send(index, source, target, device):
        pltpu.make_async_remote_copy(
            src_ref=source, dst_ref=target, send_sem=send_sems.at[index], recv_sem=recv_sems.at[index],
            device_id=device, device_id_type=MESH,
        ).start()

    def wait(view, sem):
        pltpu.make_async_copy(view, view, sem).wait()

    def arrived(index, view):
        wait(view, recv_sems.at[index])

    def total(buffer, count):
        value = buffer[0]
        for k in range(1, count):
            value = value + buffer[k]
        return value

    def at(px, py, pcore):
        return ((py * nx + px) * 2 + pcore, c)

    def send_row(k, carry):
        peer = lax.rem(r + k, n_row)
        pltpu.make_async_remote_copy(
            src_ref=outgoing.at[peer], dst_ref=recv.at[r], send_sem=row_send, recv_sem=row_recv,
            device_id=(peer, c), device_id_type=MESH,
        ).start()
        return carry

    def send_rows():
        lax.fori_loop(1, n_row, send_row, 0)

    half_tiles = s0.shape[0]
    send(0, local.at[pl.ds((1 - core) * half_tiles, half_tiles)], s0, at(x, y, 1 - core))
    recv[r] = outgoing[r]
    arrived(0, s0)
    p0[...] = local[pl.ds(core * half_tiles, half_tiles)] + s0[...]

    tiles_x = s1.shape[1]
    for k in far_first(nx):
        px = lax.rem(x + k, nx)
        send(1, p0.at[pl.ds(px * tiles_x, tiles_x)], s1.at[x], at(px, y, core))
    s1[x] = p0[pl.ds(x * tiles_x, tiles_x)]
    arrived(1, s1.at[pl.ds(0, nx - 1)])
    p1[...] = total(s1, nx)

    tiles_y = s2.shape[1]
    for k in far_first(ny):
        py = lax.rem(y + k, ny)
        send(2, p1.at[pl.ds(py * tiles_y, tiles_y)], s2.at[y], at(x, py, core))
    s2[y] = p1[pl.ds(y * tiles_y, tiles_y)]
    arrived(2, s2.at[pl.ds(0, ny - 1)])
    p2[...] = total(s2, ny)

    for k in far_first(n_col):
        send(3, p2, s3.at[c], (r, lax.rem(c + k, n_col)))
    s3[c] = p2[...]
    send_rows()

    for load in loads[2:]:
        load.wait()
    tiles = tile_users_ref.shape[0]
    block = tile_users_ref.shape[1]
    blocks = items_ref.shape[0] // block
    items = blocks * block
    live = live_ref[0, 0]
    for t in range(tiles):
        columns = slice(t * block, (t + 1) * block)
        hit = lax.broadcasted_iota(jnp.int32, (n_recv, block), 0) == tile_users_ref[t:t + 1, :]
        hot[:, columns] = hit.astype(F32).astype(BF16)
        counts = counts_ref[t].astype(F32)
        pref = (counts > 0).astype(F32)
        alive = (t < live).astype(F32)
        for k in range(blocks):
            mine = (tile_block_ref[t] == k).astype(F32) * alive
            left[k * block:(k + 1) * block, columns] = (counts * mine).astype(BF16)
            left[items + k * block:items + (k + 1) * block, columns] = (pref * mine).astype(BF16)
    sums = dot(left[...], hot[...], NT)
    conf_all = 40.0 * sums[:items]
    conf[...] = conf_all
    high, low = split(sums[items:] + conf_all)
    rh[...] = high
    rl[...] = low

    arrived(3, s3.at[pl.ds(0, n_col - 1)])
    s4[y] = total(s3, n_col)

    for k in far_first(ny):
        send(4, s4.at[y], s4.at[y], at(x, lax.rem(y + k, ny), core))
    arrived(4, s4.at[pl.ds(0, ny - 1)])

    for k in far_first(nx):
        send(5, s4, full.at[core, x], at(lax.rem(x + k, nx), y, core))
    full[core, x] = s4[...]

    wait(recv.at[pl.ds(0, n_row - 1)], row_recv)
    arrived(5, full.at[0, pl.ds(0, nx - 1)])

    send(6, full.at[core], full.at[core], at(x, y, 1 - core))

    rows = recv[...].reshape(n_recv, width)

    def tile_part(parts):
        vh, vl = parts
        scores = dot(vh, rows, NT) + dot(vl, rows, NT)
        wh, wl = split(conf[...] * scores)
        return dot(wh, rows) + dot(wl, rows)

    start = items_ref[...]
    parts = split(start)
    resid = dot(rh[...], rows) + dot(rl[...], rows) - tile_part(parts) - 0.1 * start

    arrived(6, full.at[0])
    strips = []
    for a in range(width // 8):
        cells = []
        for h in range(per):
            t = a * per + h
            cells.append(full[t // half_tiles, t % half_tiles // tiles_x, t % tiles_x // tiles_y, t % tiles_y])
        strips.append(jnp.concatenate(cells, axis=1))
    gh, gl = split(jnp.concatenate(strips, axis=0))

    def gram_part(parts):
        vh, vl = parts
        return dot(vh, gh) + dot(vl, gh) + dot(vh, gl)

    resid = resid - gram_part(parts)
    solution = start
    direction = resid
    norm_now = jnp.sum(resid * resid, axis=1, keepdims=True)
    for step in range(ITERS):
        parts = split(direction)
        image = tile_part(parts) + gram_part(parts) + 0.1 * direction
        alpha = norm_now / jnp.sum(direction * image, axis=1, keepdims=True)
        solution = solution + alpha * direction
        if step < ITERS - 1:
            resid = resid - alpha * image
            norm_next = jnp.sum(resid * resid, axis=1, keepdims=True)
            direction = resid + norm_next / norm_now * direction
            norm_now = norm_next
    out_ref[...] = solution

    wait(outgoing.at[pl.ds(0, n_row - 1)], row_send)
    sent = (s0, s1.at[pl.ds(0, nx - 1)], s2.at[pl.ds(0, ny - 1)], s3.at[pl.ds(0, n_col - 1)], s4.at[pl.ds(0, ny - 1)],
            full.at[0, pl.ds(0, nx - 1)], full.at[0])
    for index, view in enumerate(sent):
        wait(view, send_sems.at[index])

def body(dims, user_factors, item_factors, send_rows, tile_users, tile_block, tile_counts, tile_live):
    ny, nx, n_col = dims
    n_row = ny * nx * 2
    width = user_factors.shape[1]
    slots = send_rows.shape[1]
    n_tiles = width // 8 * (width // 128)
    tiles_x = n_tiles // 2 // nx
    tiles_y = tiles_x // ny
    n_recv = n_row * slots
    columns = tile_users.shape[0] * tile_users.shape[1]
    items = item_factors.shape[0]
    operands = (user_factors, item_factors, send_rows.T, tile_users, tile_block, tile_counts, tile_live)
    places = (pltpu.VMEM, pltpu.VMEM, pltpu.VMEM, pltpu.VMEM, pltpu.SMEM, pltpu.VMEM, pltpu.SMEM)

    def cells(*lead):
        return pltpu.VMEM((*lead, 8, 128), F32)

    return pl.pallas_call(
        functools.partial(kernel, dims),
        out_shape=jax.ShapeDtypeStruct(item_factors.shape, F32),
        in_specs=[pl.BlockSpec(memory_space=pltpu.HBM)] * len(operands),
        out_specs=pl.BlockSpec(memory_space=pltpu.VMEM),
        scratch_shapes=[place(a.shape, a.dtype) for place, a in zip(places, operands)] + [
            pltpu.VMEM((n_row, slots, width), BF16),
            pltpu.VMEM((n_row, slots, width), BF16),
            cells(n_tiles),
            cells(n_tiles // 2),
            cells(n_tiles // 2),
            cells(nx, tiles_x),
            cells(tiles_x),
            cells(ny, tiles_y),
            cells(tiles_y),
            cells(n_col, tiles_y),
            cells(ny, tiles_y),
            cells(2, nx, ny, tiles_y),
            pltpu.VMEM((n_recv, columns), BF16),
            pltpu.VMEM((2 * items, columns), BF16),
            pltpu.VMEM((items, n_recv), F32),
            pltpu.VMEM((items, n_recv), BF16),
            pltpu.VMEM((items, n_recv), BF16),
            pltpu.SemaphoreType.DMA((len(operands),)),
            pltpu.SemaphoreType.DMA,
            pltpu.SemaphoreType.DMA,
            pltpu.SemaphoreType.DMA((7,)),
            pltpu.SemaphoreType.DMA((7,)),
        ],
        compiler_params=pltpu.CompilerParams(
            collective_id=0, has_side_effects=True, vmem_limit_bytes=58 * 1024 * 1024
        ),
    )(*operands)


def solution(mesh):
    n_row, n_col = mesh.shape["row"], mesh.shape["col"]
    nx = min(4, n_row // 4)
    in_specs = (
        P(("row", "col"), None),
        P(("row", "col"), None),
        P(("row", "col"), None),
        P(("row", "col"), None),
        P(("row", "col")),
        P(("row", "col"), None, None),
        P("row", "col"),
    )
    return jax.shard_map(
        functools.partial(body, (n_row // 2 // nx, nx, n_col)),
        mesh=mesh, in_specs=in_specs, out_specs=P(("row", "col"), None), check_vma=False,
    )
```

time: 67 us -> 59.1 us (0.88)
  Pallas kernels: 61.7 us -> 56.6 us
  local copies, waits for them, and re-layouts: 4.33 us -> 1.67 us
    pallas_call x1, Pallas kernels: 61.7 us -> 56.6 us  [body(): pl.pallas_call(functools.partial(kernel, dims), out_shape=jax.ShapeDtypeS...]
    unnamed x12 -> x1, local copies, waits for them, and re-layouts: 4.33 us -> 1.67 us
where the time goes in v2:
time: 59.1 us; the launch traced here: 58.9 us
  Pallas kernels  56.6 us (96%)
  local copies, waits for them, and re-layouts  1.67 us (3%)
  between operations  0.66 us (1%)
    pallas_call x1, Pallas kernels, body(): pl.pallas_call(functools.partial(kernel, dims), out_shape=jax.ShapeDtypeS...  56.6 us
    unnamed x1, local copies, waits for them, and re-layouts  1.67 us

profile of v2, /device:TPU:1, one launch (start us, length us, event | category | flops | bytes accessed | tf_op | source)
XLA Modules:
  0.0 58.9 jit_solution(2944610457905968157)
XLA Ops:
  0.7 56.6 %shard_map.73 = f32[256,256]{1,0:T(8,128)} custom-call(bf16[128,256]{1,0:T(8,128)(2,1)} %users_hbm.1, f32[256,256]{1,0:T(8,128)} %items_hbm.1, s32[16,64]{1,0:T(8,128)} %bitcast.1, s32[8,128]{1,0:T(8,128)} %tile_users_hbm.1, s32[8]{0:T(128)} %tile_block_hbm.1, s32[8,128,128]{2,1,0:T(8,128)} %counts_hbm.1, s32[1,1]{1,0:T(1,128)S(6)} %copy.9.live_hbm), custom_call_target="tpu_custom_call" | custom-call | tf_op jit(solution)/shard_map/pallas_call | solution.py:252
  57.3 1.7 %copy.10 = f32[256,256]{1,0:T(8,128)} copy(f32[256,256]{1,0:T(8,128)} %shard_map.73) | data formatting | bytes 524288

commit v3 on v2

--- a/solution.py
+++ b/solution.py
@@ -8,6 +8,7 @@
 from jax.sharding import PartitionSpec as P
 
 ITERS = 3
+FIRST = (4, 3, 5)
 MESH = pl.DeviceIdType.MESH
 F32 = jnp.float32
 BF16 = jnp.bfloat16
@@ -28,6 +29,23 @@
 
 def far_first(n):
     return sorted(range(1, n), key=lambda k: -min(k, n - k))
+
+
+def near(n):
+    return sorted({k % n for k in (2, -2, 1, -1)} - {0})
+
+
+def parted(n):
+    first = [k for k in FIRST if k < n]
+    return first, [k for k in far_first(n) if k not in first]
+
+
+def rounds(n):
+    known, steps = 2, []
+    while known < n // 2:
+        steps.append(known)
+        known *= 2
+    return steps
 
 
 def kernel(
@@ -36,7 +54,7 @@
     out_ref,
     users_ref, items_ref, wanted_ref, tile_users_ref, tile_block_ref, counts_ref, live_ref,
     outgoing, recv, local, s0, p0, s1, p1, s2, p2, s3, s4, full, hot, left, conf, rh, rl,
-    load_sems, row_send, row_recv, send_sems, recv_sems,
+    load_sems, row_send, row_recv, send_sems, recv_sems, met_y, met_z,
 ):
     ny, nx, n_col = dims
     n_row = ny * nx * 2
@@ -49,13 +67,23 @@
     slots = wanted_ref.shape[0]
     n_recv = n_row * slots
 
+    def at(px, py, pcore):
+        return ((py * nx + px) * 2 + pcore, c)
+
+    def along_x(k):
+        return at(lax.rem(x + k, nx), y, core)
+
+    def along_y(k):
+        return at(x, lax.rem(y + k, ny), core)
+
+    def along_z(k):
+        return (r, lax.rem(c + k, n_col))
+
     barrier = pltpu.get_barrier_semaphore()
-    for k in far_first(n_col):
-        pl.semaphore_signal(barrier, inc=1, device_id=(r, lax.rem(c + k, n_col)), device_id_type=MESH)
-
-    def greet_row(k, carry):
-        pl.semaphore_signal(barrier, inc=1, device_id=(lax.rem(r + k, n_row), c), device_id_type=MESH)
-        return carry
+    friends = [at(x, y, 1 - core)] + [along_x(k) for k in range(1, nx)]
+    friends += [along_y(k) for k in near(ny)] + [along_z(k) for k in near(n_col)]
+    for friend in friends:
+        pl.semaphore_signal(barrier, inc=1, device_id=friend, device_id_type=MESH)
 
     loads = [
         pltpu.make_async_copy(source, target, load_sems.at[i])
@@ -66,9 +94,7 @@
     ]
     for load in loads:
         load.start()
-    lax.fori_loop(1, n_row, greet_row, 0)
     loads[0].wait()
-    loads[1].wait()
 
     per = width // 128
     u = users_ref[...]
@@ -77,12 +103,14 @@
         for h in range(per):
             local[a * per + h] = gram[8 * a:8 * a + 8, 128 * h:128 * h + 128]
 
-    wanted = wanted_ref[...].T[:, :, None]
-    pick = (wanted == lax.broadcasted_iota(jnp.int32, (n_row, slots, rows_dev), 2)).astype(F32)
-    rows_out = dot(pick.reshape(n_recv, rows_dev).astype(BF16), u).astype(BF16)
-    outgoing[...] = rows_out.reshape(n_row, slots, width)
-
-    pl.semaphore_wait(barrier, n_row - 1 + n_col - 1)
+    pl.semaphore_wait(barrier, len(friends))
+
+    def meet(semaphores, i, n, along):
+        for k in (rounds(n)[i], n - rounds(n)[i]):
+            pl.semaphore_signal(semaphores.at[i], inc=1, device_id=along(k), device_id_type=MESH)
+
+    def met(semaphores, i):
+        pl.semaphore_wait(semaphores.at[i], 2)
 
     def send(index, source, target, device):
         pltpu.make_async_remote_copy(
@@ -102,46 +130,64 @@
             value = value + buffer[k]
         return value
 
-    def at(px, py, pcore):
-        return ((py * nx + px) * 2 + pcore, c)
-
-    def send_row(k, carry):
-        peer = lax.rem(r + k, n_row)
-        pltpu.make_async_remote_copy(
-            src_ref=outgoing.at[peer], dst_ref=recv.at[r], send_sem=row_send, recv_sem=row_recv,
-            device_id=(peer, c), device_id_type=MESH,
-        ).start()
-        return carry
-
-    def send_rows():
-        lax.fori_loop(1, n_row, send_row, 0)
+    def send_rows(steps):
+        side = 2 * nx
+        for step in steps:
+            def one(k, carry):
+                peer = lax.rem(y + step, ny) * side + lax.rem(lax.rem(r, side) + k, side)
+                pltpu.make_async_remote_copy(
+                    src_ref=outgoing.at[peer], dst_ref=recv.at[r], send_sem=row_send, recv_sem=row_recv,
+                    device_id=(peer, c), device_id_type=MESH,
+                ).start()
+                return carry
+
+            lax.fori_loop(0 if step else 1, side, one, 0)
+
+    first, second = parted(ny)
 
     half_tiles = s0.shape[0]
     send(0, local.at[pl.ds((1 - core) * half_tiles, half_tiles)], s0, at(x, y, 1 - core))
-    recv[r] = outgoing[r]
+    if rounds(ny):
+        meet(met_y, 0, ny, along_y)
+    if rounds(n_col):
+        meet(met_z, 0, n_col, along_z)
     arrived(0, s0)
     p0[...] = local[pl.ds(core * half_tiles, half_tiles)] + s0[...]
 
     tiles_x = s1.shape[1]
     for k in far_first(nx):
         px = lax.rem(x + k, nx)
-        send(1, p0.at[pl.ds(px * tiles_x, tiles_x)], s1.at[x], at(px, y, core))
+        send(1, p0.at[pl.ds(px * tiles_x, tiles_x)], s1.at[x], along_x(k))
     s1[x] = p0[pl.ds(x * tiles_x, tiles_x)]
+    for i in range(1, len(rounds(n_col))):
+        met(met_z, i - 1)
+        meet(met_z, i, n_col, along_z)
     arrived(1, s1.at[pl.ds(0, nx - 1)])
     p1[...] = total(s1, nx)
 
+    if rounds(ny):
+        met(met_y, 0)
     tiles_y = s2.shape[1]
     for k in far_first(ny):
         py = lax.rem(y + k, ny)
-        send(2, p1.at[pl.ds(py * tiles_y, tiles_y)], s2.at[y], at(x, py, core))
+        send(2, p1.at[pl.ds(py * tiles_y, tiles_y)], s2.at[y], along_y(k))
     s2[y] = p1[pl.ds(y * tiles_y, tiles_y)]
+    loads[1].wait()
+    wanted = wanted_ref[...].T[:, :, None]
+    pick = (wanted == lax.broadcasted_iota(jnp.int32, (n_row, slots, rows_dev), 2)).astype(F32)
+    rows_out = dot(pick.reshape(n_recv, rows_dev).astype(BF16), u).astype(BF16)
+    outgoing[...] = rows_out.reshape(n_row, slots, width)
+    recv[r] = outgoing[r]
+    send_rows([0])
     arrived(2, s2.at[pl.ds(0, ny - 1)])
     p2[...] = total(s2, ny)
 
+    if rounds(n_col):
+        met(met_z, len(rounds(n_col)) - 1)
     for k in far_first(n_col):
-        send(3, p2, s3.at[c], (r, lax.rem(c + k, n_col)))
+        send(3, p2, s3.at[c], along_z(k))
     s3[c] = p2[...]
-    send_rows()
+    send_rows(first)
 
     for load in loads[2:]:
         load.wait()
@@ -149,7 +195,7 @@
     block = tile_users_ref.shape[1]
     blocks = items_ref.shape[0] // block
     items = blocks * block
-    live = live_ref[0, 0]
+    live = live_ref[0]
     for t in range(tiles):
         columns = slice(t * block, (t + 1) * block)
         hit = lax.broadcasted_iota(jnp.int32, (n_recv, block), 0) == tile_users_ref[t:t + 1, :]
@@ -172,17 +218,19 @@
     s4[y] = total(s3, n_col)
 
     for k in far_first(ny):
-        send(4, s4.at[y], s4.at[y], at(x, lax.rem(y + k, ny), core))
+        send(4, s4.at[y], s4.at[y], along_y(k))
+    send_rows(second)
     arrived(4, s4.at[pl.ds(0, ny - 1)])
 
     for k in far_first(nx):
-        send(5, s4, full.at[core, x], at(lax.rem(x + k, nx), y, core))
+        send(5, s4, full.at[core, x], along_x(k))
     full[core, x] = s4[...]
 
+    arrived(5, full.at[0, pl.ds(0, nx - 1)])
+
+    send(6, full.at[core], full.at[core], at(x, y, 1 - core))
+
     wait(recv.at[pl.ds(0, n_row - 1)], row_recv)
-    arrived(5, full.at[0, pl.ds(0, nx - 1)])
-
-    send(6, full.at[core], full.at[core], at(x, y, 1 - core))
 
     rows = recv[...].reshape(n_recv, width)
 
@@ -243,7 +291,7 @@
     n_recv = n_row * slots
     columns = tile_users.shape[0] * tile_users.shape[1]
     items = item_factors.shape[0]
-    operands = (user_factors, item_factors, send_rows.T, tile_users, tile_block, tile_counts, tile_live)
+    operands = (user_factors, item_factors, send_rows.T, tile_users, tile_block, tile_counts, tile_live.reshape(1))
     places = (pltpu.VMEM, pltpu.VMEM, pltpu.VMEM, pltpu.VMEM, pltpu.SMEM, pltpu.VMEM, pltpu.SMEM)
 
     def cells(*lead):
@@ -251,7 +299,7 @@
 
     return pl.pallas_call(
         functools.partial(kernel, dims),
-        out_shape=jax.ShapeDtypeStruct(item_factors.shape, F32),
+        out_shape=pltpu.VMEM(item_factors.shape, F32),
         in_specs=[pl.BlockSpec(memory_space=pltpu.HBM)] * len(operands),
         out_specs=pl.BlockSpec(memory_space=pltpu.VMEM),
         scratch_shapes=[place(a.shape, a.dtype) for place, a in zip(places, operands)] + [
@@ -277,6 +325,8 @@
             pltpu.SemaphoreType.DMA,
             pltpu.SemaphoreType.DMA((7,)),
             pltpu.SemaphoreType.DMA((7,)),
+            pltpu.SemaphoreType.REGULAR((max(1, len(rounds(ny))),)),
+            pltpu.SemaphoreType.REGULAR((max(1, len(rounds(n_col))),)),
         ],
         compiler_params=pltpu.CompilerParams(
             collective_id=0, has_side_effects=True, vmem_limit_bytes=58 * 1024 * 1024

time: 59.1 us -> 53.9 us (0.912)
  Pallas kernels: 56.6 us -> 52.3 us
  local copies, waits for them, and re-layouts: 1.67 us -> 0.71 us
    pallas_call x1, Pallas kernels: 56.6 us -> 52.3 us  [body(): pl.pallas_call(functools.partial(kernel, dims), out_shape=pltpu.VMEM(item...]
    unnamed x1, local copies, waits for them, and re-layouts: 1.67 us -> 0.71 us
where the time goes in v3:
time: 53.9 us; the launch traced here: 53.7 us
  Pallas kernels  52.3 us (97%)
  local copies, waits for them, and re-layouts  0.71 us (1%)
  between operations  0.66 us (1%)
    pallas_call x1, Pallas kernels, body(): pl.pallas_call(functools.partial(kernel, dims), out_shape=pltpu.VMEM(item...  52.3 us

profile of v3, /device:TPU:1, one launch (start us, length us, event | category | flops | bytes accessed | tf_op | source)
XLA Modules:
  0.0 53.7 jit_solution(8560547377545489937)
XLA Ops:
  0.7 52.3 %shard_map.73 = f32[256,256]{1,0:T(8,128)S(1)} custom-call(bf16[128,256]{1,0:T(8,128)(2,1)} %users_hbm.1, f32[256,256]{1,0:T(8,128)} %items_hbm.1, s32[16,64]{1,0:T(8,128)} %bitcast.3, s32[8,128]{1,0:T(8,128)} %tile_users_hbm.1, s32[8]{0:T(128)} %tile_block_hbm.1, s32[8,128,128]{2,1,0:T(8,128)} %counts_hbm.1, s32[1]{0:T(128)} %bitcast.2.live_hbm), custom_call_target="tpu_custom_call" | custom-call | tf_op jit(solution)/shard_map/pallas_call | solution.py:300
  53.0 0.7 %copy.9 = f32[256,256]{1,0:T(8,128)} copy(f32[256,256]{1,0:T(8,128)S(1)} %shard_map.73) | data formatting | bytes 524288

commit v4 on v3

--- a/solution.py
+++ b/solution.py
@@ -9,6 +9,7 @@
 
 ITERS = 3
 FIRST = (4, 3, 5)
+CHUNKS = 4
 MESH = pl.DeviceIdType.MESH
 F32 = jnp.float32
 BF16 = jnp.bfloat16
@@ -25,6 +26,16 @@
 def split(x):
     high = x.astype(BF16)
     return high, (x - high.astype(F32)).astype(BF16)
+
+
+def stacked(x):
+    return jnp.concatenate(split(x), axis=0)
+
+
+def dot_stacked(parts, b, dims=NN):
+    both = dot(parts, b, dims)
+    half = both.shape[0] // 2
+    return both[:half] + both[half:]
 
 
 def far_first(n):
@@ -79,12 +90,6 @@
     def along_z(k):
         return (r, lax.rem(c + k, n_col))
 
-    barrier = pltpu.get_barrier_semaphore()
-    friends = [at(x, y, 1 - core)] + [along_x(k) for k in range(1, nx)]
-    friends += [along_y(k) for k in near(ny)] + [along_z(k) for k in near(n_col)]
-    for friend in friends:
-        pl.semaphore_signal(barrier, inc=1, device_id=friend, device_id_type=MESH)
-
     loads = [
         pltpu.make_async_copy(source, target, load_sems.at[i])
         for i, (source, target) in enumerate((
@@ -92,7 +97,15 @@
             (tile_block_hbm, tile_block_ref), (live_hbm, live_ref), (counts_hbm, counts_ref),
         ))
     ]
-    for load in loads:
+    loads[0].start()
+
+    barrier = pltpu.get_barrier_semaphore()
+    friends = [at(x, y, 1 - core)] + [along_x(k) for k in range(1, nx)]
+    friends += [along_y(k) for k in near(ny)] + [along_z(k) for k in near(n_col)]
+    for friend in friends:
+        pl.semaphore_signal(barrier, inc=1, device_id=friend, device_id_type=MESH)
+
+    for load in loads[1:]:
         load.start()
     loads[0].wait()
 
@@ -215,68 +228,81 @@
     rl[...] = low
 
     arrived(3, s3.at[pl.ds(0, n_col - 1)])
-    s4[y] = total(s3, n_col)
+    here = pl.ds(y * tiles_y, tiles_y)
+    s4[here] = total(s3, n_col)
 
     for k in far_first(ny):
-        send(4, s4.at[y], s4.at[y], along_y(k))
+        send(4, s4.at[here], s4.at[here], along_y(k))
     send_rows(second)
-    arrived(4, s4.at[pl.ds(0, ny - 1)])
-
+    arrived(4, s4.at[pl.ds(0, (ny - 1) * tiles_y)])
+
+    mine = pl.ds((core * nx + x) * tiles_x, tiles_x)
     for k in far_first(nx):
-        send(5, s4, full.at[core, x], along_x(k))
-    full[core, x] = s4[...]
-
-    arrived(5, full.at[0, pl.ds(0, nx - 1)])
-
-    send(6, full.at[core], full.at[core], at(x, y, 1 - core))
+        for other in (core, 1 - core):
+            send(5, s4, full.at[mine], at(lax.rem(x + k, nx), y, other))
+    send(5, s4, full.at[mine], at(x, y, 1 - core))
+    full[mine] = s4[...]
 
     wait(recv.at[pl.ds(0, n_row - 1)], row_recv)
 
     rows = recv[...].reshape(n_recv, width)
 
+    def pieces():
+        step = n_recv // CHUNKS
+        return [slice(k * step, (k + 1) * step) for k in range(CHUNKS)]
+
     def tile_part(parts):
-        vh, vl = parts
-        scores = dot(vh, rows, NT) + dot(vl, rows, NT)
-        wh, wl = split(conf[...] * scores)
-        return dot(wh, rows) + dot(wl, rows)
+        image = None
+        for piece in pieces():
+            some = rows[piece]
+            share = dot_stacked(stacked(conf[:, piece] * dot_stacked(parts, some, NT)), some)
+            image = share if image is None else image + share
+        return image
+
+    def tile_curve(parts):
+        curve = None
+        for piece in pieces():
+            share = jnp.sum(conf[:, piece] * jnp.square(dot_stacked(parts, rows[piece], NT)), axis=1, keepdims=True)
+            curve = share if curve is None else curve + share
+        return curve
 
     start = items_ref[...]
-    parts = split(start)
+    parts = stacked(start)
     resid = dot(rh[...], rows) + dot(rl[...], rows) - tile_part(parts) - 0.1 * start
 
-    arrived(6, full.at[0])
+    arrived(5, full.at[pl.ds(0, (2 * nx - 1) * tiles_x)])
     strips = []
     for a in range(width // 8):
-        cells = []
-        for h in range(per):
-            t = a * per + h
-            cells.append(full[t // half_tiles, t % half_tiles // tiles_x, t % tiles_x // tiles_y, t % tiles_y])
-        strips.append(jnp.concatenate(cells, axis=1))
+        strips.append(jnp.concatenate([full[a * per + h] for h in range(per)], axis=1))
     gh, gl = split(jnp.concatenate(strips, axis=0))
 
     def gram_part(parts):
-        vh, vl = parts
-        return dot(vh, gh) + dot(vl, gh) + dot(vh, gl)
+        return dot_stacked(parts, gh) + dot(parts[:items], gl)
 
     resid = resid - gram_part(parts)
     solution = start
     direction = resid
     norm_now = jnp.sum(resid * resid, axis=1, keepdims=True)
     for step in range(ITERS):
-        parts = split(direction)
-        image = tile_part(parts) + gram_part(parts) + 0.1 * direction
+        parts = stacked(direction)
+        image = gram_part(parts) + 0.1 * direction
+        if step == ITERS - 1:
+            curve = jnp.sum(direction * image, axis=1, keepdims=True)
+            curve = curve + tile_curve(parts)
+            out_ref[...] = solution + norm_now / curve * direction
+            break
+        image = image + tile_part(parts)
         alpha = norm_now / jnp.sum(direction * image, axis=1, keepdims=True)
         solution = solution + alpha * direction
-        if step < ITERS - 1:
-            resid = resid - alpha * image
-            norm_next = jnp.sum(resid * resid, axis=1, keepdims=True)
-            direction = resid + norm_next / norm_now * direction
-            norm_now = norm_next
-    out_ref[...] = solution
+        resid = resid - alpha * image
+        norm_next = jnp.sum(resid * resid, axis=1, keepdims=True)
+        direction = resid + norm_next / norm_now * direction
+        norm_now = norm_next
 
     wait(outgoing.at[pl.ds(0, n_row - 1)], row_send)
-    sent = (s0, s1.at[pl.ds(0, nx - 1)], s2.at[pl.ds(0, ny - 1)], s3.at[pl.ds(0, n_col - 1)], s4.at[pl.ds(0, ny - 1)],
-            full.at[0, pl.ds(0, nx - 1)], full.at[0])
+    sent = [s0, s1.at[pl.ds(0, nx - 1)], s2.at[pl.ds(0, ny - 1)], s3.at[pl.ds(0, n_col - 1)],
+            s4.at[pl.ds(0, (ny - 1) * tiles_y)]]
+    sent += [full.at[pl.ds(0, (2 * nx - 1) * tiles_x)]]
     for index, view in enumerate(sent):
         wait(view, send_sems.at[index])
 
@@ -313,8 +339,8 @@
             cells(ny, tiles_y),
             cells(tiles_y),
             cells(n_col, tiles_y),
-            cells(ny, tiles_y),
-            cells(2, nx, ny, tiles_y),
+            cells(tiles_x),
+            cells(n_tiles),
             pltpu.VMEM((n_recv, columns), BF16),
             pltpu.VMEM((2 * items, columns), BF16),
             pltpu.VMEM((items, n_recv), F32),

time: 53.9 us -> 51.9 us (0.963)
  Pallas kernels: 52.3 us -> 50.4 us
    pallas_call x1, Pallas kernels: 52.3 us -> 50.4 us  [body(): pl.pallas_call(functools.partial(kernel, dims), out_shape=pltpu.VMEM(item...]
where the time goes in v4:
time: 51.9 us; the launch traced here: 51.7 us
  Pallas kernels  50.4 us (97%)
  local copies, waits for them, and re-layouts  0.71 us (1%)
  between operations  0.66 us (1%)
    pallas_call x1, Pallas kernels, body(): pl.pallas_call(functools.partial(kernel, dims), out_shape=pltpu.VMEM(item...  50.4 us

profile of v4, /device:TPU:1, one launch (start us, length us, event | category | flops | bytes accessed | tf_op | source)
XLA Modules:
  0.0 51.7 jit_solution(5486583545634670288)
XLA Ops:
  0.7 50.4 %shard_map.73 = f32[256,256]{1,0:T(8,128)S(1)} custom-call(bf16[128,256]{1,0:T(8,128)(2,1)} %users_hbm.1, f32[256,256]{1,0:T(8,128)} %items_hbm.1, s32[16,64]{1,0:T(8,128)} %bitcast.3, s32[8,128]{1,0:T(8,128)} %tile_users_hbm.1, s32[8]{0:T(128)} %tile_block_hbm.1, s32[8,128,128]{2,1,0:T(8,128)} %counts_hbm.1, s32[1]{0:T(128)} %bitcast.2.live_hbm), custom_call_target="tpu_custom_call" | custom-call | tf_op jit(solution)/shard_map/pallas_call | solution.py:326
  51.0 0.7 %copy.9 = f32[256,256]{1,0:T(8,128)} copy(f32[256,256]{1,0:T(8,128)S(1)} %shard_map.73) | data formatting | bytes 524288

commit v5 on v4

--- a/solution.py
+++ b/solution.py
@@ -8,7 +8,7 @@
 from jax.sharding import PartitionSpec as P
 
 ITERS = 3
-FIRST = (4, 3, 5)
+FIRST = (5, 4, 3, 1)
 CHUNKS = 4
 MESH = pl.DeviceIdType.MESH
 F32 = jnp.float32
@@ -145,16 +145,19 @@
 
     def send_rows(steps):
         side = 2 * nx
-        for step in steps:
-            def one(k, carry):
-                peer = lax.rem(y + step, ny) * side + lax.rem(lax.rem(r, side) + k, side)
+        j = lax.rem(r, side)
+
+        def one(k, carry):
+            for step in steps:
+                peer = lax.rem(y + step, ny) * side + lax.rem(j + k, side)
                 pltpu.make_async_remote_copy(
                     src_ref=outgoing.at[peer], dst_ref=recv.at[r], send_sem=row_send, recv_sem=row_recv,
                     device_id=(peer, c), device_id_type=MESH,
                 ).start()
-                return carry
-
-            lax.fori_loop(0 if step else 1, side, one, 0)
+            return carry
+
+        if steps:
+            lax.fori_loop(1 if 0 in steps else 0, side, one, 0)
 
     first, second = parted(ny)
 

time: 51.9 us -> 51.7 us (level)
  no operation moved by 1% of the time
where the time goes in v5:
time: 51.7 us; the launch traced here: 51.6 us
  Pallas kernels  50.2 us (97%)
  local copies, waits for them, and re-layouts  0.71 us (1%)
  between operations  0.66 us (1%)
    pallas_call x1, Pallas kernels, body(): pl.pallas_call(functools.partial(kernel, dims), out_shape=pltpu.VMEM(item...  50.2 us

profile of v5, /device:TPU:1, one launch (start us, length us, event | category | flops | bytes accessed | tf_op | source)
XLA Modules:
  0.0 51.6 jit_solution(9848321537720989448)
XLA Ops:
  0.7 50.2 %shard_map.73 = f32[256,256]{1,0:T(8,128)S(1)} custom-call(bf16[128,256]{1,0:T(8,128)(2,1)} %users_hbm.1, f32[256,256]{1,0:T(8,128)} %items_hbm.1, s32[16,64]{1,0:T(8,128)} %bitcast.3, s32[8,128]{1,0:T(8,128)} %tile_users_hbm.1, s32[8]{0:T(128)} %tile_block_hbm.1, s32[8,128,128]{2,1,0:T(8,128)} %counts_hbm.1, s32[1]{0:T(128)} %bitcast.2.live_hbm), custom_call_target="tpu_custom_call" | custom-call | tf_op jit(solution)/shard_map/pallas_call | solution.py:329
  50.9 0.7 %copy.9 = f32[256,256]{1,0:T(8,128)} copy(f32[256,256]{1,0:T(8,128)S(1)} %shard_map.73) | data formatting | bytes 524288

commit v6 on v5

--- a/solution.py
+++ b/solution.py
@@ -42,8 +42,8 @@
     return sorted(range(1, n), key=lambda k: -min(k, n - k))
 
 
-def near(n):
-    return sorted({k % n for k in (2, -2, 1, -1)} - {0})
+def near(n, reach=2):
+    return sorted({k % n for k in range(-reach, reach + 1)} - {0})
 
 
 def parted(n):
@@ -51,8 +51,8 @@
     return first, [k for k in far_first(n) if k not in first]
 
 
-def rounds(n):
-    known, steps = 2, []
+def rounds(n, known=2):
+    steps = []
     while known < n // 2:
         steps.append(known)
         known *= 2
@@ -101,7 +101,7 @@
 
     barrier = pltpu.get_barrier_semaphore()
     friends = [at(x, y, 1 - core)] + [along_x(k) for k in range(1, nx)]
-    friends += [along_y(k) for k in near(ny)] + [along_z(k) for k in near(n_col)]
+    friends += [along_y(k) for k in near(ny)] + [along_z(k) for k in near(n_col, 4)]
     for friend in friends:
         pl.semaphore_signal(barrier, inc=1, device_id=friend, device_id_type=MESH)
 
@@ -119,7 +119,7 @@
     pl.semaphore_wait(barrier, len(friends))
 
     def meet(semaphores, i, n, along):
-        for k in (rounds(n)[i], n - rounds(n)[i]):
+        for k in (rounds(n, 2 if n == ny else 4)[i], n - rounds(n, 2 if n == ny else 4)[i]):
             pl.semaphore_signal(semaphores.at[i], inc=1, device_id=along(k), device_id_type=MESH)
 
     def met(semaphores, i):
@@ -165,7 +165,7 @@
     send(0, local.at[pl.ds((1 - core) * half_tiles, half_tiles)], s0, at(x, y, 1 - core))
     if rounds(ny):
         meet(met_y, 0, ny, along_y)
-    if rounds(n_col):
+    if rounds(n_col, 4):
         meet(met_z, 0, n_col, along_z)
     arrived(0, s0)
     p0[...] = local[pl.ds(core * half_tiles, half_tiles)] + s0[...]
@@ -175,7 +175,7 @@
         px = lax.rem(x + k, nx)
         send(1, p0.at[pl.ds(px * tiles_x, tiles_x)], s1.at[x], along_x(k))
     s1[x] = p0[pl.ds(x * tiles_x, tiles_x)]
-    for i in range(1, len(rounds(n_col))):
+    for i in range(1, len(rounds(n_col, 4))):
         met(met_z, i - 1)
         meet(met_z, i, n_col, along_z)
     arrived(1, s1.at[pl.ds(0, nx - 1)])
@@ -198,8 +198,8 @@
     arrived(2, s2.at[pl.ds(0, ny - 1)])
     p2[...] = total(s2, ny)
 
-    if rounds(n_col):
-        met(met_z, len(rounds(n_col)) - 1)
+    if rounds(n_col, 4):
+        met(met_z, len(rounds(n_col, 4)) - 1)
     for k in far_first(n_col):
         send(3, p2, s3.at[c], along_z(k))
     s3[c] = p2[...]
@@ -355,7 +355,7 @@
             pltpu.SemaphoreType.DMA((7,)),
             pltpu.SemaphoreType.DMA((7,)),
             pltpu.SemaphoreType.REGULAR((max(1, len(rounds(ny))),)),
-            pltpu.SemaphoreType.REGULAR((max(1, len(rounds(n_col))),)),
+            pltpu.SemaphoreType.REGULAR((max(1, len(rounds(n_col, 4))),)),
         ],
         compiler_params=pltpu.CompilerParams(
             collective_id=0, has_side_effects=True, vmem_limit_bytes=58 * 1024 * 1024

time: 51.7 us -> 51.8 us (level)
  no operation moved by 1% of the time
where the time goes in v6:
time: 51.8 us; the launch traced here: 51.6 us
  Pallas kernels  50.3 us (97%)
  local copies, waits for them, and re-layouts  0.71 us (1%)
  between operations  0.66 us (1%)
    pallas_call x1, Pallas kernels, body(): pl.pallas_call(functools.partial(kernel, dims), out_shape=pltpu.VMEM(item...  50.3 us

profile of v6, /device:TPU:1, one launch (start us, length us, event | category | flops | bytes accessed | tf_op | source)
XLA Modules:
  0.0 51.6 jit_solution(7453233400462330697)
XLA Ops:
  0.7 50.3 %shard_map.73 = f32[256,256]{1,0:T(8,128)S(1)} custom-call(bf16[128,256]{1,0:T(8,128)(2,1)} %users_hbm.1, f32[256,256]{1,0:T(8,128)} %items_hbm.1, s32[16,64]{1,0:T(8,128)} %bitcast.3, s32[8,128]{1,0:T(8,128)} %tile_users_hbm.1, s32[8]{0:T(128)} %tile_block_hbm.1, s32[8,128,128]{2,1,0:T(8,128)} %counts_hbm.1, s32[1]{0:T(128)} %bitcast.2.live_hbm), custom_call_target="tpu_custom_call" | custom-call | tf_op jit(solution)/shard_map/pallas_call | solution.py:329
  50.9 0.7 %copy.9 = f32[256,256]{1,0:T(8,128)} copy(f32[256,256]{1,0:T(8,128)S(1)} %shard_map.73) | data formatting | bytes 524288
